TPU v7x, 32 devices: a whole 2x2x4 slice. The times are simulated.
32 devices in a mesh: rep: 2 (over y), exp: 16 (over z, x, core).
Axes of the slice: x: 2, y: 2, z: 4, core: 2. Of those that a mesh axis runs over, the one named last changes fastest.
Arguments:
- tokens: bfloat16 [4096, 1024], P(('rep', 'exp')), may hold values from -6 to 6
- cotangent: bfloat16 [4096, 1024], P(('rep', 'exp')), may hold values from -6 to 6
- expert_ids: int32 [4096, 2], P(('rep', 'exp')), may hold values from 0 to 15, all different within a row; in each aligned block of 128 rows (0 to 127, 128 to 255, ...) at most 32 rows name the same one
- combine_weight: float32 [4096, 2], P(('rep', 'exp')), may hold values from 0.2 to 1
- gate_weight: bfloat16 [16, 1024, 768], P('exp', 'rep'), may hold values from -0.1875 to 0.1875
- up_weight: bfloat16 [16, 1024, 768], P('exp', 'rep'), may hold values from -0.1875 to 0.1875
- down_weight: bfloat16 [16, 768, 1024], P('exp', None, 'rep'), may hold values from -0.21875 to 0.21875
Outputs:
- mixed: bfloat16 [4096, 1024], P(('rep', 'exp'))
- token_grad: bfloat16 [4096, 1024], P(('rep', 'exp'))
- gate_grad: bfloat16 [16, 1024, 768], P('exp', 'rep')
- up_grad: bfloat16 [16, 1024, 768], P('exp', 'rep')
- down_grad: bfloat16 [16, 768, 1024], P('exp', None, 'rep')
Inputs may be any that keep to these rules, and one draw needn't show every extreme that they name: `expert_ids`: each token names 2 different experts. Among the 128 tokens of one aligned block of rows, no expert is named more than 32 times, and in some block an expert is named exactly 32 times.
All inputs are finite; a program needn't handle non-finite values.
Results may differ from a plain program's by a relative error of at most 0.014.
Values may be sent and summed in bfloat16 or wider, within the bound.
A program may use at most 64 MiB of HBM per device.

v0:
```python
import jax
import jax.numpy as jnp
from jax import lax
from jax.sharding import PartitionSpec as P


def slot_rows(block_ids, expert_count, capacity):
    flat = block_ids.reshape(-1)
    onehot = (flat[:, None] == jnp.arange(expert_count, dtype=jnp.int32)[None, :]).astype(jnp.int32)
    before = jnp.cumsum(onehot, axis=0) - onehot
    return flat * capacity + jnp.sum(before * onehot, axis=1)


def expert_forward(block_x, w_gate, w_up, w_down):
    gate_value = jnp.dot(block_x, w_gate, preferred_element_type=jnp.float32)
    up_value = jnp.dot(block_x, w_up, preferred_element_type=jnp.float32)
    swish_value = jax.nn.silu(gate_value)
    hidden = (swish_value * up_value).astype(jnp.bfloat16)
    output = jnp.dot(hidden, w_down, preferred_element_type=jnp.float32).astype(jnp.bfloat16)
    return (gate_value, up_value, swish_value, hidden, output)


def average_rows(received, replicas):
    features, hidden_units = received.shape
    stacked = received.reshape(replicas, features // replicas, hidden_units).astype(jnp.float32)
    return (jnp.sum(stacked, axis=0) / replicas).astype(jnp.bfloat16)


def per_device(tokens, cotangent, expert_ids, combine_weight, gate_weight, up_weight, down_weight):
    tok_rows, features = tokens.shape
    top_count = expert_ids.shape[1]
    groups = lax.axis_size("exp")
    replicas = lax.axis_size("rep")
    capacity = 2 * tok_rows * top_count // groups
    pair_count = tok_rows * top_count
    destination = slot_rows(expert_ids, groups, capacity)
    x_pairs = jnp.repeat(tokens, top_count, axis=0)
    cot_pairs = (combine_weight[:, :, None] * cotangent[:, None, :].astype(jnp.float32)).astype(
        jnp.bfloat16
    )
    cot_pairs = cot_pairs.reshape(pair_count, features)
    send_rows = jnp.zeros((groups * capacity, features), jnp.bfloat16).at[destination].set(x_pairs)
    send_cot = jnp.zeros((groups * capacity, features), jnp.bfloat16).at[destination].set(cot_pairs)
    w_gate, w_up, w_down = (
        lax.all_gather(gate_weight[0], "rep", axis=0, tiled=True),
        lax.all_gather(up_weight[0], "rep", axis=0, tiled=True),
        lax.all_gather(down_weight[0], "rep", axis=1, tiled=True),
    )
    recv_rows, recv_cot = (
        lax.all_to_all(send_rows, "exp", split_axis=0, concat_axis=0, tiled=True),
        lax.all_to_all(send_cot, "exp", split_axis=0, concat_axis=0, tiled=True),
    )
    gate_value, up_value, swish_value, hidden, output = expert_forward(
        recv_rows, w_gate, w_up, w_down
    )
    grad_hidden = lax.dot_general(
        recv_cot, w_down, (((1,), (1,)), ((), ())), preferred_element_type=jnp.float32
    )
    sigma = jax.nn.sigmoid(gate_value)
    grad_gate = (grad_hidden * up_value * sigma * (1.0 + gate_value * (1.0 - sigma))).astype(
        jnp.bfloat16
    )
    grad_up = (grad_hidden * swish_value).astype(jnp.bfloat16)
    grad_rows = (
        lax.dot_general(
            grad_gate, w_gate, (((1,), (1,)), ((), ())), preferred_element_type=jnp.float32
        )
        + lax.dot_general(
            grad_up, w_up, (((1,), (1,)), ((), ())), preferred_element_type=jnp.float32
        )
    ).astype(jnp.bfloat16)
    back_out, back_grad = (
        lax.all_to_all(output, "exp", split_axis=0, concat_axis=0, tiled=True),
        lax.all_to_all(grad_rows, "exp", split_axis=0, concat_axis=0, tiled=True),
    )
    part_gate = lax.dot_general(
        recv_rows, grad_gate, (((0,), (0,)), ((), ())), preferred_element_type=jnp.float32
    ).astype(jnp.bfloat16)
    part_up = lax.dot_general(
        recv_rows, grad_up, (((0,), (0,)), ((), ())), preferred_element_type=jnp.float32
    ).astype(jnp.bfloat16)
    part_down = lax.dot_general(
        recv_cot, hidden, (((0,), (0,)), ((), ())), preferred_element_type=jnp.float32
    ).astype(jnp.bfloat16)
    red_gate, red_up, red_down = (
        lax.all_to_all(part_gate, "rep", split_axis=0, concat_axis=0, tiled=True),
        lax.all_to_all(part_up, "rep", split_axis=0, concat_axis=0, tiled=True),
        lax.all_to_all(part_down, "rep", split_axis=0, concat_axis=0, tiled=True),
    )
    gate_grad = average_rows(red_gate, replicas)[None]
    up_grad = average_rows(red_up, replicas)[None]
    down_grad = average_rows(red_down, replicas).T[None]
    out_pairs = back_out[destination].reshape(tok_rows, top_count, features).astype(jnp.float32)
    mixed = jnp.sum(combine_weight[:, :, None] * out_pairs, axis=1).astype(jnp.bfloat16)
    grad_pairs = back_grad[destination].reshape(tok_rows, top_count, features).astype(jnp.float32)
    token_grad = jnp.sum(grad_pairs, axis=1).astype(jnp.bfloat16)
    return (mixed, token_grad, gate_grad, up_grad, down_grad)


def solution(mesh):
    placed = (
        P(("rep", "exp"), None),
        P(("rep", "exp"), None),
        P(("rep", "exp"), None),
        P(("rep", "exp"), None),
        P("exp", "rep", None),
        P("exp", "rep", None),
        P("exp", None, "rep"),
    )
    return jax.shard_map(
        per_device,
        mesh=mesh,
        in_specs=placed,
        out_specs=(
            P(("rep", "exp"), None),
            P(("rep", "exp"), None),
            P("exp", "rep", None),
            P("exp", "rep", None),
            P("exp", None, "rep"),
        ),
        check_vma=False,
    )
```

profile of v0, /device:TPU:0, one launch (start us, length us, event | category | flops | bytes accessed | tf_op | source)
XLA Modules:
  0.0 243.7 jit_solution(6499297918243497780)
XLA Ops:
  7.2 0.0 all-gather.9.cloned.1.call-start
  7.2 0.7 all-gather.9.cloned.1.call-update
  7.9 0.8 copy.15
  8.7 0.1 eq.29
  8.8 0.1 eq.25
  9.0 0.6 reduce-window.6
  9.6 0.2 slice_reduce_fusion
  9.8 0.7 broadcast_multiply_fusion
  10.5 0.1 copy.14
  10.6 0.1 mul.70
  10.7 1.2 broadcast_in_dim.4
  12.0 0.2 reshape.141
  12.2 0.1 fusion.25
  12.3 2.6 %scatter_custom_fusion = bf16[512,1024]{1,0:T(8,128)(2,1)} fusion(s32[256]{0:T(256)S(1)} %bitcast.81, bf16[256,1024]{1,0:T(8,128)(2,1)S(1)} %reshape.141, bf16[]{:T(256)} %constant.8.clone.1), kind=kCustom, calls=%fused_computation.39 | custom fusion | bytes 1048578 | tf_op jit(solution)/shard_map/scatter | solution.py:42
  14.9 7.5 %all-to-all-start = ((bf16[16,32,1024]{2,1,0:T(8,128)(2,1)}), bf16[16,32,1024]{2,1,0:T(8,128)(2,1)S(1)}, u32[]{:S(2)}, u32[]{:S(2)}) async-start(bf16[16,32,1024]{2,1,0:T(8,128)(2,1)} %bitcast.3), calls=%async_computation | async-start | bytes 2097152 | tf_op jit(solution)/shard_map/all_to_all | solution.py:50
  22.4 0.0 all-gather.7.cloned.1.call-start
  22.4 0.7 all-gather.7.cloned.1.call-update
  23.2 0.1 copy.13
  23.3 0.1 mul.75
  23.4 0.3 mul.77
  23.7 0.7 mul.78
  24.4 2.8 %scatter_custom_fusion.1 = bf16[512,1024]{1,0:T(8,128)(2,1)} fusion(s32[256]{0:T(256)S(1)} %bitcast.82, f32[256,1024]{1,0:T(8,128)S(1)} %mul.78, f32[256]{0:T(256)S(1)} %mul.75, bf16[]{:T(256)} %constant.8.clone.1), kind=kCustom, calls=%fused_computation.36 | custom fusion | flops 524288 | bytes 2098178 | tf_op jit(solution)/shard_map/scatter | solution.py:43
  27.3 18.1 %all-to-all-done = bf16[16,32,1024]{2,1,0:T(8,128)(2,1)S(1)} async-done(((bf16[16,32,1024]{2,1,0:T(8,128)(2,1)}), bf16[16,32,1024]{2,1,0:T(8,128)(2,1)S(1)}, u32[]{:S(2)}, u32[]{:S(2)}) %all-to-all-start) | async-done | bytes 1048608 | tf_op jit(solution)/shard_map/all_to_all | solution.py:50
  45.3 6.9 %all-to-all-start.2 = ((bf16[16,32,1024]{2,1,0:T(8,128)(2,1)}), bf16[16,32,1024]{2,1,0:T(8,128)(2,1)S(1)}, u32[]{:S(2)}, u32[]{:S(2)}) async-start(bf16[16,32,1024]{2,1,0:T(8,128)(2,1)} %bitcast.10), calls=%async_computation.2 | async-start | bytes 2097152 | tf_op jit(solution)/shard_map/all_to_all | solution.py:51
  52.2 0.0 all-gather.11.cloned.1.call-start
  52.3 0.7 all-gather.11.cloned.1.call-update
  53.0 0.0 all-gather.9.cloned.1.call-done
  53.0 3.5 %fusion.5 = f32[512,768]{1,0:T(8,128)} fusion(bf16[512,1024]{1,0:T(8,128)(2,1)S(1)} %bitcast.75, bf16[1,1024,768]{2,1,0:T(8,128)(2,1)} %all-gather.9.cloned.1.call-done), kind=kOutput, calls=%fused_computation.16 | convolution fusion | flops 805306368 | bytes 4194304 | tf_op jit(solution)/shard_map/dot_general | solution.py:16
  56.5 11.8 %all-gather.7.cloned.1.call-done = bf16[1,1024,768]{2,1,0:T(8,128)(2,1)} async-done(((bf16[1,512,768]{2,1,0:T(8,128)(2,1)}), bf16[1,1024,768]{2,1,0:T(8,128)(2,1)}) %all-gather.7.cloned.1.call-update) | async-done | bytes 1572880 | tf_op jit(solution)/shard_map/all_gather | solution.py:45
  68.3 3.6 %fusion.9 = f32[512,768]{1,0:T(8,128)} fusion(bf16[512,1024]{1,0:T(8,128)(2,1)S(1)} %bitcast.76, bf16[1,1024,768]{2,1,0:T(8,128)(2,1)} %all-gather.7.cloned.1.call-done), kind=kOutput, calls=%fused_computation.20 | convolution fusion | flops 805306368 | bytes 4194304 | tf_op jit(solution)/shard_map/dot_general | solution.py:15
  71.8 25.2 %all-gather.11.cloned.1.call-done = bf16[1,768,1024]{2,1,0:T(8,128)(2,1)} async-done(((bf16[1,768,512]{2,1,0:T(8,128)(2,1)}), bf16[1,768,1024]{2,1,0:T(8,128)(2,1)}) %all-gather.11.cloned.1.call-update) | async-done | bytes 1572880 | tf_op jit(solution)/shard_map/all_gather | solution.py:47
  97.1 5.4 %multiply_convert_fusion.3 = (bf16[512,768]{1,0:T(8,128)(2,1)}, bf16[512,768]{1,0:T(8,128)(2,1)S(1)}, bf16[512,768]{1,0:T(8,128)(2,1)}) fusion(f32[512,768]{1,0:T(8,128)} %fusion.9, f32[512,768]{1,0:T(8,128)} %fusion.5, bf16[512,1024]{1,0:T(8,128)(2,1)S(1)} %bitcast.79, bf16[1,768,1024]{2,1,0:T(8,128)(2,1)} %all-gather.11.cloned.1.call-done), kind=kOutput, calls=%fused_computation.25 | convolution fusion | flops 811204608 | bytes 8126464 | tf_op jit(solution)/shard_map/dot_general | solution.py:56
  102.5 2.2 convolution_convert_fusion.2
  104.7 3.7 %all-to-all-start.4 = ((bf16[2,512,768]{2,1,0:T(8,128)(2,1)}), bf16[2,512,768]{2,1,0:T(8,128)(2,1)S(1)}, u32[]{:S(2)}, u32[]{:S(2)}) async-start(bf16[2,512,768]{2,1,0:T(8,128)(2,1)} %bitcast.14), calls=%async_computation.4 | async-start | bytes 3145728 | tf_op jit(solution)/shard_map/all_to_all | solution.py:86
  108.3 3.3 %convolution_convert_fusion.1 = bf16[1024,768]{1,0:T(8,128)(2,1)} fusion(bf16[512,1024]{1,0:T(8,128)(2,1)S(1)} %bitcast.78, bf16[512,768]{1,0:T(8,128)(2,1)} %get-tuple-element.10), kind=kOutput, calls=%fused_computation.9 | convolution fusion | flops 806092800 | bytes 3407872 | tf_op jit(solution)/shard_map/dot_general | solution.py:79
  111.6 16.2 %all-to-all-done.4 = bf16[2,512,768]{2,1,0:T(8,128)(2,1)S(1)} async-done(((bf16[2,512,768]{2,1,0:T(8,128)(2,1)}), bf16[2,512,768]{2,1,0:T(8,128)(2,1)S(1)}, u32[]{:S(2)}, u32[]{:S(2)}) %all-to-all-start.4) | async-done | bytes 1572896 | tf_op jit(solution)/shard_map/all_to_all | solution.py:86
  127.8 1.2 copy-done
  129.0 3.9 %all-to-all-start.5 = ((bf16[2,512,768]{2,1,0:T(8,128)(2,1)}), bf16[2,512,768]{2,1,0:T(8,128)(2,1)S(1)}, u32[]{:S(2)}, u32[]{:S(2)}) async-start(bf16[2,512,768]{2,1,0:T(8,128)(2,1)} %bitcast.74), calls=%async_computation.5 | async-start | bytes 3145728 | tf_op jit(solution)/shard_map/all_to_all | solution.py:87
  132.8 3.7 %convolution_convert_fusion = bf16[1024,768]{1,0:T(8,128)(2,1)} fusion(bf16[512,1024]{1,0:T(8,128)(2,1)} %bitcast.80, bf16[512,768]{1,0:T(8,128)(2,1)} %get-tuple-element.12), kind=kOutput, calls=%fused_computation.8 | convolution fusion | flops 806092800 | bytes 3407872 | tf_op jit(solution)/shard_map/dot_general | solution.py:82
  136.5 14.7 %all-to-all-done.5 = bf16[2,512,768]{2,1,0:T(8,128)(2,1)S(1)} async-done(((bf16[2,512,768]{2,1,0:T(8,128)(2,1)}), bf16[2,512,768]{2,1,0:T(8,128)(2,1)S(1)}, u32[]{:S(2)}, u32[]{:S(2)}) %all-to-all-start.5) | async-done | bytes 1572896 | tf_op jit(solution)/shard_map/all_to_all | solution.py:87
  151.3 1.1 copy-done.1
  152.4 3.7 %all-to-all-start.6 = ((bf16[2,512,768]{2,1,0:T(8,128)(2,1)}), bf16[2,512,768]{2,1,0:T(8,128)(2,1)S(1)}, u32[]{:S(2)}, u32[]{:S(2)}) async-start(bf16[2,512,768]{2,1,0:T(8,128)(2,1)} %bitcast.73), calls=%async_computation.6 | async-start | bytes 3145728 | tf_op jit(solution)/shard_map/all_to_all | solution.py:88
  156.1 2.8 %fusion.7 = f32[512,1024]{1,0:T(8,128)S(1)} fusion(bf16[512,768]{1,0:T(8,128)(2,1)} %copy-done.10, bf16[1,1024,768]{2,1,0:T(8,128)(2,1)} %all-gather.7.cloned.1.call-done), kind=kOutput, calls=%fused_computation.18 | convolution fusion | flops 805306368 | bytes 4456448 | tf_op jit(solution)/shard_map/dot_general | solution.py:65
  158.9 2.0 add_convert_fusion
  160.9 12.8 %all-to-all-done.6 = bf16[2,512,768]{2,1,0:T(8,128)(2,1)S(1)} async-done(((bf16[2,512,768]{2,1,0:T(8,128)(2,1)}), bf16[2,512,768]{2,1,0:T(8,128)(2,1)S(1)}, u32[]{:S(2)}, u32[]{:S(2)}) %all-to-all-start.6) | async-done | bytes 1572896 | tf_op jit(solution)/shard_map/all_to_all | solution.py:88
  173.8 1.2 copy-done.3
  174.9 5.6 %all-to-all-start.3 = ((bf16[16,32,1024]{2,1,0:T(8,128)(2,1)}), bf16[16,32,1024]{2,1,0:T(8,128)(2,1)S(1)}, u32[]{:S(2)}, u32[]{:S(2)}) async-start(bf16[16,32,1024]{2,1,0:T(8,128)(2,1)} %bitcast.12), calls=%async_computation.3 | async-start | bytes 2097152 | tf_op jit(solution)/shard_map/all_to_all | solution.py:74
  180.6 3.1 %fusion.12 = bf16[512,1024]{1,0:T(8,128)(2,1)} fusion(bf16[512,768]{1,0:T(8,128)(2,1)} %get-tuple-element.12, bf16[1,768,1024]{2,1,0:T(8,128)(2,1)S(1)} %copy-done.8), kind=kOutput, calls=%fused_computation.30 | convolution fusion | flops 805830656 | bytes 3407872 | tf_op jit(solution)/shard_map/dot_general | solution.py:19
  183.6 19.9 %all-to-all-done.3 = bf16[16,32,1024]{2,1,0:T(8,128)(2,1)S(1)} async-done(((bf16[16,32,1024]{2,1,0:T(8,128)(2,1)}), bf16[16,32,1024]{2,1,0:T(8,128)(2,1)S(1)}, u32[]{:S(2)}, u32[]{:S(2)}) %all-to-all-start.3) | async-done | bytes 1048608 | tf_op jit(solution)/shard_map/all_to_all | solution.py:74
  203.5 6.9 %all-to-all-start.1 = ((bf16[16,32,1024]{2,1,0:T(8,128)(2,1)}), bf16[16,32,1024]{2,1,0:T(8,128)(2,1)S(1)}, u32[]{:S(2)}, u32[]{:S(2)}) async-start(bf16[16,32,1024]{2,1,0:T(8,128)(2,1)} %bitcast.8), calls=%async_computation.1 | async-start | bytes 2097152 | tf_op jit(solution)/shard_map/all_to_all | solution.py:73
  210.4 1.9 convert_reduce_fusion
  212.2 0.1 fusion.17
  212.4 1.2 copy.19
  213.5 2.0 convert_reduce_fusion.2
  215.5 0.3 convert_reduce_fusion.1
  215.8 1.0 fusion.15
  216.8 1.0 fusion.16
  217.7 1.2 gather_fusion.1
  218.9 0.2 reshape.119
  219.1 2.1 reduce_sum.62
  221.2 12.1 %all-to-all-done.1 = bf16[16,32,1024]{2,1,0:T(8,128)(2,1)S(1)} async-done(((bf16[16,32,1024]{2,1,0:T(8,128)(2,1)}), bf16[16,32,1024]{2,1,0:T(8,128)(2,1)S(1)}, u32[]{:S(2)}, u32[]{:S(2)}) %all-to-all-start.1) | async-done | bytes 1048608 | tf_op jit(solution)/shard_map/all_to_all | solution.py:73
  233.3 1.2 gather_fusion
  234.5 0.7 reshape.120
  235.1 2.1 multiply_reduce_fusion
  (25 shorter events, 0.1 us)
Async XLA Ops:
  7.2 45.8 %all-gather.9.cloned.1.call-start = ((), (), s32[]{:S(2)}) async-start(), calls=%async_computation.8 | async-start | bytes 2359296 | tf_op jit(solution)/shard_map/all_gather | solution.py:46
  14.9 8.3 %copy-start.6 = (f32[128,2]{0,1:T(2,128)S(1)}, f32[128,2]{0,1:T(2,128)}, u32[]{:S(2)}) copy-start(f32[128,2]{0,1:T(2,128)} %param.10) | copy-start | bytes 3076
  14.9 8.5 %copy-start.5 = (bf16[128,1024]{1,0:T(8,128)(2,1)S(1)}, bf16[128,1024]{1,0:T(8,128)(2,1)}, u32[]{:S(2)}) copy-start(bf16[128,1024]{1,0:T(8,128)(2,1)} %param.8) | copy-start | bytes 786436
  14.9 30.4 %all-to-all-start = ((bf16[16,32,1024]{2,1,0:T(8,128)(2,1)}), bf16[16,32,1024]{2,1,0:T(8,128)(2,1)S(1)}, u32[]{:S(2)}, u32[]{:S(2)}) async-start(bf16[16,32,1024]{2,1,0:T(8,128)(2,1)} %bitcast.3), calls=%async_computation | async-start | bytes 2097152 | tf_op jit(solution)/shard_map/all_to_all | solution.py:50
  22.4 45.9 %all-gather.7.cloned.1.call-start = ((), (), s32[]{:S(2)}) async-start(), calls=%async_computation.7 | async-start | bytes 2359296 | tf_op jit(solution)/shard_map/all_gather | solution.py:45
  45.3 51.7 %all-to-all-start.2 = ((bf16[16,32,1024]{2,1,0:T(8,128)(2,1)}), bf16[16,32,1024]{2,1,0:T(8,128)(2,1)S(1)}, u32[]{:S(2)}, u32[]{:S(2)}) async-start(bf16[16,32,1024]{2,1,0:T(8,128)(2,1)} %bitcast.10), calls=%async_computation.2 | async-start | bytes 2097152 | tf_op jit(solution)/shard_map/all_to_all | solution.py:51
  52.2 44.9 %all-gather.11.cloned.1.call-start = ((), (), s32[]{:S(2)}) async-start(), calls=%async_computation.9 | async-start | bytes 2359296 | tf_op jit(solution)/shard_map/all_gather | solution.py:47
  97.1 5.4 %copy-start.4 = (bf16[16,32,1024]{2,1,0:T(8,128)(2,1)}, bf16[16,32,1024]{2,1,0:T(8,128)(2,1)S(1)}, u32[]{:S(2)}) copy-start(bf16[16,32,1024]{2,1,0:T(8,128)(2,1)S(1)} %all-to-all-done.2) | copy-start | bytes 3145732
  102.5 2.2 copy-start.10
  104.7 23.2 %all-to-all-start.4 = ((bf16[2,512,768]{2,1,0:T(8,128)(2,1)}), bf16[2,512,768]{2,1,0:T(8,128)(2,1)S(1)}, u32[]{:S(2)}, u32[]{:S(2)}) async-start(bf16[2,512,768]{2,1,0:T(8,128)(2,1)} %bitcast.14), calls=%async_computation.4 | async-start | bytes 3145728 | tf_op jit(solution)/shard_map/all_to_all | solution.py:86
  127.8 1.2 copy-start
  129.0 22.3 %all-to-all-start.5 = ((bf16[2,512,768]{2,1,0:T(8,128)(2,1)}), bf16[2,512,768]{2,1,0:T(8,128)(2,1)S(1)}, u32[]{:S(2)}, u32[]{:S(2)}) async-start(bf16[2,512,768]{2,1,0:T(8,128)(2,1)} %bitcast.74), calls=%async_computation.5 | async-start | bytes 3145728 | tf_op jit(solution)/shard_map/all_to_all | solution.py:87
  151.3 1.1 copy-start.1
  152.4 21.4 %all-to-all-start.6 = ((bf16[2,512,768]{2,1,0:T(8,128)(2,1)}), bf16[2,512,768]{2,1,0:T(8,128)(2,1)S(1)}, u32[]{:S(2)}, u32[]{:S(2)}) async-start(bf16[2,512,768]{2,1,0:T(8,128)(2,1)} %bitcast.73), calls=%async_computation.6 | async-start | bytes 3145728 | tf_op jit(solution)/shard_map/all_to_all | solution.py:88
  156.1 2.8 %copy-start.7 = (bf16[1,1024,768]{2,1,0:T(8,128)(2,1)S(1)}, bf16[1,1024,768]{2,1,0:T(8,128)(2,1)}, u32[]{:S(2)}) copy-start(bf16[1,1024,768]{2,1,0:T(8,128)(2,1)} %all-gather.9.cloned.1.call-done) | copy-start | bytes 4718596
  156.1 2.8 %copy-start.9 = (bf16[512,768]{1,0:T(8,128)(2,1)S(1)}, bf16[512,768]{1,0:T(8,128)(2,1)}, u32[]{:S(2)}) copy-start(bf16[512,768]{1,0:T(8,128)(2,1)} %get-tuple-element.10) | copy-start | bytes 2359300
  160.9 19.6 %copy-start.8 = (bf16[1,768,1024]{2,1,0:T(8,128)(2,1)S(1)}, bf16[1,768,1024]{2,1,0:T(8,128)(2,1)}, u32[]{:S(2)}) copy-start(bf16[1,768,1024]{2,1,0:T(8,128)(2,1)} %all-gather.11.cloned.1.call-done) | copy-start | bytes 4718596
  173.7 1.2 copy-start.3
  174.9 28.6 %all-to-all-start.3 = ((bf16[16,32,1024]{2,1,0:T(8,128)(2,1)}), bf16[16,32,1024]{2,1,0:T(8,128)(2,1)S(1)}, u32[]{:S(2)}, u32[]{:S(2)}) async-start(bf16[16,32,1024]{2,1,0:T(8,128)(2,1)} %bitcast.12), calls=%async_computation.3 | async-start | bytes 2097152 | tf_op jit(solution)/shard_map/all_to_all | solution.py:74
  203.5 29.8 %all-to-all-start.1 = ((bf16[16,32,1024]{2,1,0:T(8,128)(2,1)}), bf16[16,32,1024]{2,1,0:T(8,128)(2,1)S(1)}, u32[]{:S(2)}, u32[]{:S(2)}) async-start(bf16[16,32,1024]{2,1,0:T(8,128)(2,1)} %bitcast.8), calls=%async_computation.1 | async-start | bytes 2097152 | tf_op jit(solution)/shard_map/all_to_all | solution.py:73
  213.5 2.0 copy-start.2
Sparse Core Ops, SparseCore 0:
  9.5 29.8 all-gather.8
  41.0 27.2 all-gather.6
  69.8 27.2 all-gather.10
where the time goes:
time: 246 us; the launch traced here: 244 us
  waiting for transfers between devices  133 us (54%)
  starting transfers between devices  38.2 us (16%)
  matrix products  29.5 us (12%)
  local copies, waits for them, and re-layouts  14.6 us (6%)
  other arithmetic  14.6 us (6%)
  between operations  14 us (6%)
    all_gather x1, waiting for transfers between devices, per_device(): lax.all_gather(down_weight[0], 'rep', axis=1, tiled=True)  25.2 us
    all_to_all x1, waiting for transfers between devices, per_device(): lax.all_to_all(grad_rows, 'exp', split_axis=0, concat_axis=0, tiled=True)  19.9 us
    all_to_all x1, waiting for transfers between devices, per_device(): lax.all_to_all(send_rows, 'exp', split_axis=0, concat_axis=0, tiled=True)  18.1 us
    all_to_all x1, waiting for transfers between devices, per_device(): lax.all_to_all(part_gate, 'rep', split_axis=0, concat_axis=0, tiled=True)  16.2 us
    all_to_all x1, waiting for transfers between devices, per_device(): lax.all_to_all(part_up, 'rep', split_axis=0, concat_axis=0, tiled=True)  14.7 us
    all_to_all x1, waiting for transfers between devices, per_device(): lax.all_to_all(part_down, 'rep', split_axis=0, concat_axis=0, tiled=True)  12.8 us
    all_to_all x1, waiting for transfers between devices, per_device(): lax.all_to_all(output, 'exp', split_axis=0, concat_axis=0, tiled=True)  12.1 us
    all_gather x1, waiting for transfers between devices, per_device(): lax.all_gather(gate_weight[0], 'rep', axis=0, tiled=True)  11.8 us
  transfers between devices with their start and end apart: 10, of which 8 were waited for; matrix products, arithmetic and copies ran while one was open for 18% of the time, Pallas kernels for 0%

commit v1 on v0

v1 whole, which is shorter than its diff:
```python
import functools

import jax
import jax.numpy as jnp
from jax import lax
from jax.experimental import pallas as pl
from jax.experimental.pallas import tpu as pltpu
from jax.sharding import PartitionSpec as P

MESH = pl.DeviceIdType.MESH
F32, BF16 = jnp.float32, jnp.bfloat16
NN = (((1,), (0,)), ((), ()))
NT = (((1,), (1,)), ((), ()))
TN = (((0,), (0,)), ((), ()))


def mm(a, b, dims):
    return lax.dot_general(a, b, dims, preferred_element_type=F32)


def rows_2d(block):
    groups, capacity, features = block.shape
    if capacity % 16:
        return block.astype(F32).reshape(groups * capacity, features).astype(BF16)
    return block.reshape(groups * capacity, features)


def kernel(
    reps, groups, cap, width,
    tok, cot, ids, cw, wg, wu, wd,
    mixed, token_grad, gate_grad, up_grad, down_grad,
    send_x, send_c, send_o, send_d, recv_x, recv_c, recv_o, recv_d,
    full_g, full_u, full_d, hid, d_gate, d_up,
    part_g, part_u, part_d, red_g, red_u, red_d,
    pick, pick_hi, pick_lo,
    a_send, a_recv, w_send, w_recv, g_send, g_recv, local_sem,
):
    rep, exp = lax.axis_index("rep"), lax.axis_index("exp")
    tokens, features = tok.shape
    share, hidden = wg.shape
    chunks = hidden // width
    rows = groups * cap
    mine = pl.ds(pl.multiple_of(rep * share, share), share)

    def cols(c):
        if isinstance(c, int):
            return pl.ds(c * width, width)
        return pl.ds(pl.multiple_of(c * width, width), width)

    barrier = pltpu.get_barrier_semaphore()

    def greet(i, carry):
        pl.semaphore_signal(
            barrier, inc=1, device_id=(rep, lax.rem(exp + i, groups)), device_id_type=MESH
        )
        return carry

    lax.fori_loop(1, groups, greet, 0)
    for j in range(1, reps):
        pl.semaphore_signal(
            barrier, inc=1, device_id=(lax.rem(rep + j, reps), exp), device_id_type=MESH
        )

    own_copies = [
        pltpu.make_async_copy(wg, full_g.at[mine, :], local_sem.at[0]),
        pltpu.make_async_copy(wu, full_u.at[mine, :], local_sem.at[1]),
        pltpu.make_async_copy(wd, full_d.at[:, mine], local_sem.at[2]),
    ]
    for copy in own_copies:
        copy.start()

    lanes = 128
    expert = lax.broadcasted_iota(jnp.int32, (tokens, lanes), 1)
    id_val = ids[...]
    cw_val = cw[...]
    hot = [(id_val[:, k : k + 1] == expert).astype(F32) for k in range(2)]
    earlier = (
        lax.broadcasted_iota(jnp.int32, (tokens, tokens), 1)
        < lax.broadcasted_iota(jnp.int32, (tokens, tokens), 0)
    )
    before = mm(earlier.astype(F32).astype(BF16), (hot[0] + hot[1]).astype(BF16), NN)
    place = before + (expert * cap).astype(F32)
    dest = [jnp.sum(hot[k] * place, axis=1, keepdims=True) for k in range(2)]
    table = jnp.where(
        expert == 0, dest[0],
        jnp.where(expert == 1, dest[1],
                  jnp.where(expert == 2, cw_val[:, 0:1],
                            jnp.where(expert == 3, cw_val[:, 1:2], 0.0))),
    )
    flipped = jnp.transpose(table)
    down_rows = lax.broadcasted_iota(jnp.int32, (rows, tokens), 0).astype(F32)
    sel0 = (down_rows == flipped[0:1, :]).astype(F32)
    sel1 = (down_rows == flipped[1:2, :]).astype(F32)
    select = (sel0 + sel1).astype(BF16)
    row_weight = jnp.sum(
        sel0 * flipped[2:3, :] + sel1 * flipped[3:4, :], axis=1, keepdims=True
    )
    send_x[...] = mm(select, tok[...], NN).reshape(groups, cap, features).astype(BF16)

    pl.semaphore_wait(barrier, groups - 1 + reps - 1)

    def weight_copy(a, c, j):
        peer = lax.rem(rep + j, reps)
        src, dst = (
            (wg, full_g), (wu, full_u), (wd, full_d)
        )[a]
        if a < 2:
            src, dst = src.at[:, cols(c)], dst.at[mine, cols(c)]
        else:
            src, dst = src.at[cols(c), :], dst.at[cols(c), mine]
        return pltpu.make_async_remote_copy(
            src_ref=src, dst_ref=dst,
            send_sem=w_send.at[j - 1, a, c], recv_sem=w_recv.at[j - 1, a, c],
            device_id=(peer, exp), device_id_type=MESH,
        )

    def grad_copy(a, c, j):
        peer = lax.rem(rep + j, reps)
        theirs = pl.ds(pl.multiple_of(peer * share, share), share)
        src, dst = ((part_g, red_g), (part_u, red_u), (part_d, red_d))[a]
        if a < 2:
            src, dst = src.at[theirs, cols(c)], dst.at[j - 1, :, cols(c)]
        else:
            src, dst = src.at[cols(c), theirs], dst.at[j - 1, cols(c), :]
        return pltpu.make_async_remote_copy(
            src_ref=src, dst_ref=dst,
            send_sem=g_send.at[j - 1, a, c], recv_sem=g_recv.at[j - 1, a, c],
            device_id=(peer, exp), device_id_type=MESH,
        )

    exchange = ((send_x, recv_x), (send_c, recv_c), (send_o, recv_o), (send_d, recv_d))

    def row_copy(kind, i):
        peer = lax.rem(exp + i, groups)
        src, dst = exchange[kind]
        return pltpu.make_async_remote_copy(
            src_ref=src.at[peer], dst_ref=dst.at[exp],
            send_sem=a_send.at[kind, i - 1], recv_sem=a_recv.at[kind, i - 1],
            device_id=(rep, peer), device_id_type=MESH,
        )

    def start_rows(kind):
        def step(i, carry):
            row_copy(kind, i).start()
            return carry

        lax.fori_loop(1, groups, step, 0)
        src, dst = exchange[kind]
        pltpu.make_async_copy(src.at[exp], dst.at[exp], local_sem.at[3 + kind]).start()

    def finish_rows(kind):
        def step(i, carry):
            row_copy(kind, i).wait_recv()
            return carry

        lax.fori_loop(1, groups, step, 0)
        src, dst = exchange[kind]
        pltpu.make_async_copy(src.at[exp], dst.at[exp], local_sem.at[3 + kind]).wait()

    for c in range(chunks):
        for a in range(3):
            for j in range(1, reps):
                weight_copy(a, c, j).start()
    start_rows(0)
    send_c[...] = (
        (mm(select, cot[...], NN) * row_weight).reshape(groups, cap, features).astype(BF16)
    )
    start_rows(1)

    across = lax.broadcasted_iota(jnp.int32, (tokens, rows), 1).astype(F32)
    at0 = (across == dest[0]).astype(F32)
    at1 = (across == dest[1]).astype(F32)
    pick[...] = (at0 + at1).astype(BF16)
    weighted = at0 * cw_val[:, 0:1] + at1 * cw_val[:, 1:2]
    high = weighted.astype(BF16)
    pick_hi[...] = high
    pick_lo[...] = (weighted - high.astype(F32)).astype(BF16)

    for copy in own_copies:
        copy.wait()
    finish_rows(0)
    finish_rows(1)

    def chunk(c, carry):
        x = rows_2d(recv_x[...])
        for j in range(1, reps):
            for a in range(3):
                weight_copy(a, c, j).wait_recv()
        gate = mm(x, full_g[:, cols(c)], NN)
        up = mm(x, full_u[:, cols(c)], NN)
        cots = rows_2d(recv_c[...])
        grad_h = mm(cots, full_d[cols(c), :], NT)
        sigma = jax.nn.sigmoid(gate)
        swish = gate * sigma
        h = (swish * up).astype(BF16)
        dg = (grad_h * up * sigma * (1.0 + gate * (1.0 - sigma))).astype(BF16)
        du = (grad_h * swish).astype(BF16)
        hid[:, cols(c)] = h
        d_gate[:, cols(c)] = dg
        d_up[:, cols(c)] = du
        part_g[:, cols(c)] = mm(x, dg, TN).astype(BF16)
        for j in range(1, reps):
            grad_copy(0, c, j).start()
        part_u[:, cols(c)] = mm(x, du, TN).astype(BF16)
        for j in range(1, reps):
            grad_copy(1, c, j).start()
        part_d[cols(c), :] = mm(h, cots, TN).astype(BF16)
        for j in range(1, reps):
            grad_copy(2, c, j).start()
        return carry

    lax.fori_loop(0, chunks, chunk, 0)

    send_o[...] = mm(hid[...], full_d[...], NN).reshape(groups, cap, features).astype(BF16)
    start_rows(2)
    send_d[...] = (
        (mm(d_gate[...], full_g[...], NT) + mm(d_up[...], full_u[...], NT))
        .reshape(groups, cap, features)
        .astype(BF16)
    )
    start_rows(3)

    finish_rows(2)
    back = rows_2d(recv_o[...])
    mixed[...] = (mm(pick_hi[...], back, NN) + mm(pick_lo[...], back, NN)).astype(BF16)
    finish_rows(3)
    token_grad[...] = mm(pick[...], rows_2d(recv_d[...]), NN).astype(BF16)

    for c in range(chunks):
        for a in range(3):
            for j in range(1, reps):
                grad_copy(a, c, j).wait_recv()
            own, red, out = (
                (part_g, red_g, gate_grad), (part_u, red_u, up_grad), (part_d, red_d, down_grad)
            )[a]
            if a < 2:
                total = own[mine, cols(c)].astype(F32)
                for j in range(1, reps):
                    total = total + red[j - 1, :, cols(c)].astype(F32)
                out[:, cols(c)] = (total / reps).astype(BF16)
            else:
                total = own[cols(c), mine].astype(F32)
                for j in range(1, reps):
                    total = total + red[j - 1, cols(c), :].astype(F32)
                out[cols(c), :] = (total / reps).astype(BF16)

    for c in range(chunks):
        for a in range(3):
            for j in range(1, reps):
                weight_copy(a, c, j).wait_send()
                grad_copy(a, c, j).wait_send()

    def sent(i, carry):
        for kind in range(4):
            row_copy(kind, i).wait_send()
        return carry

    lax.fori_loop(1, groups, sent, 0)


def per_device(reps, groups, tokens, cotangent, expert_ids, combine_weight, gate_w, up_w, down_w):
    tok_rows, features = tokens.shape
    top = expert_ids.shape[1]
    share, hidden = gate_w.shape[1:]
    cap = 2 * tok_rows * top // groups
    rows = groups * cap
    width = 256
    chunks = hidden // width
    vmem = pl.BlockSpec(memory_space=pltpu.VMEM)
    block = pltpu.VMEM((groups, cap, features), BF16)
    act = pltpu.VMEM((rows, hidden), BF16)
    dma = pltpu.SemaphoreType.DMA
    others = reps - 1
    outs = pl.pallas_call(
        functools.partial(kernel, reps, groups, cap, width),
        out_shape=(
            jax.ShapeDtypeStruct((tok_rows, features), BF16),
            jax.ShapeDtypeStruct((tok_rows, features), BF16),
            jax.ShapeDtypeStruct((share, hidden), BF16),
            jax.ShapeDtypeStruct((share, hidden), BF16),
            jax.ShapeDtypeStruct((hidden, share), BF16),
        ),
        in_specs=[vmem] * 7,
        out_specs=(vmem,) * 5,
        scratch_shapes=[block] * 8
        + [
            pltpu.VMEM((features, hidden), BF16),
            pltpu.VMEM((features, hidden), BF16),
            pltpu.VMEM((hidden, features), BF16),
        ]
        + [act] * 3
        + [
            pltpu.VMEM((features, hidden), BF16),
            pltpu.VMEM((features, hidden), BF16),
            pltpu.VMEM((hidden, features), BF16),
            pltpu.VMEM((others, share, hidden), BF16),
            pltpu.VMEM((others, share, hidden), BF16),
            pltpu.VMEM((others, hidden, share), BF16),
        ]
        + [pltpu.VMEM((tok_rows, rows), BF16)] * 3
        + [
            dma((4, groups - 1)),
            dma((4, groups - 1)),
            dma((others, 3, chunks)),
            dma((others, 3, chunks)),
            dma((others, 3, chunks)),
            dma((others, 3, chunks)),
            dma((7,)),
        ],
        compiler_params=pltpu.CompilerParams(
            collective_id=0, has_side_effects=True, vmem_limit_bytes=56 * 1024 * 1024
        ),
        cost_estimate=pl.CostEstimate(
            flops=18 * rows * features * hidden,
            bytes_accessed=16 * share * hidden,
            transcendentals=rows * hidden,
        ),
    )(tokens, cotangent, expert_ids, combine_weight, gate_w[0], up_w[0], down_w[0])
    mixed, token_grad, gate_grad, up_grad, down_grad = outs
    return mixed, token_grad, gate_grad[None], up_grad[None], down_grad[None]


def solution(mesh):
    placed = (
        P(("rep", "exp"), None),
        P(("rep", "exp"), None),
        P(("rep", "exp"), None),
        P(("rep", "exp"), None),
        P("exp", "rep", None),
        P("exp", "rep", None),
        P("exp", None, "rep"),
    )
    return jax.shard_map(
        functools.partial(per_device, mesh.shape["rep"], mesh.shape["exp"]),
        mesh=mesh,
        in_specs=placed,
        out_specs=(
            P(("rep", "exp"), None),
            P(("rep", "exp"), None),
            P("exp", "rep", None),
            P("exp", "rep", None),
            P("exp", None, "rep"),
        ),
        check_vma=False,
    )
```

time: 246 us -> 125 us (0.51)
  waiting for transfers between devices: 133 us -> 0 us
  Pallas kernels: 0 us -> 115 us
  starting transfers between devices: 38.2 us -> 0 us
  matrix products: 29.5 us -> 0 us
  other arithmetic: 14.6 us -> 0 us
  between operations: 14 us -> 0.66 us
  local copies, waits for them, and re-layouts: 14.6 us -> 9.28 us
    pallas_call x0 -> x1, Pallas kernels: none -> 115 us  [per_device(): pl.pallas_call(functools.partial(kernel, reps, groups, cap, width), out_s...]
    all_to_all x7 -> x0, waiting for transfers between devices: 93.8 us -> none  [the longest x1 19.9 us: per_device(): lax.all_to_all(grad_rows, 'exp', split_axis=0, concat_axis=0, tiled=True)]
    all_to_all x7 -> x0, starting transfers between devices: 38 us -> none  [the longest x1 7.49 us: per_device(): lax.all_to_all(send_rows, 'exp', split_axis=0, concat_axis=0, tiled=True)]
    all_gather x3 -> x0, waiting for transfers between devices: 37 us -> none  [the longest x1 25.2 us: per_device(): lax.all_gather(down_weight[0], 'rep', axis=1, tiled=True)]
    dot_general x9 -> x0, matrix products: 29.5 us -> none  [the longest x1 5.39 us: per_device(): lax.dot_general(recv_cot, w_down, (((1,), (1,)), ((), ())), preferred_ele...]
    reduce_sum x6 -> x0, other arithmetic: 8.34 us -> none  [the longest x3 4.09 us: average_rows(): return (jnp.sum(stacked, axis=0) / replicas).astype(jnp.bfloat16)]
    unnamed x25 -> x17, local copies, waits for them, and re-layouts: 5.56 us -> 9.28 us
    scatter x1 -> x0, other arithmetic: 2.83 us -> none  [per_device(): jnp.zeros((groups * capacity, features), jnp.bfloat16).at[destination]]
  transfers between devices with their start and end apart: 10 -> 0, of which waited for: 8 -> 0; matrix products, arithmetic and copies ran while one was open for 18% -> 0% of each run, Pallas kernels for 0% -> 0%
where the time goes in v1:
time: 125 us
  Pallas kernels  115 us (92%)
  local copies, waits for them, and re-layouts  9.28 us (7%)
    pallas_call x1, Pallas kernels, per_device(): pl.pallas_call(functools.partial(kernel, reps, groups, cap, width), out_s...  115 us
    unnamed x17, local copies, waits for them, and re-layouts  9.28 us

profile of v1, /device:TPU:0, one launch (start us, length us, event | category | flops | bytes accessed | tf_op | source)
XLA Modules:
  0.0 124.7 jit_solution(16874393716724914692)
XLA Ops:
  0.6 0.0 copy-start.3
  0.6 0.7 copy-done.3
  1.3 0.0 copy-start.4
  1.3 0.7 copy.12.ids
  2.1 0.0 copy-done.4
  2.1 0.7 copy.13.cw
  2.8 114.7 %shard_map.110 = (bf16[128,1024]{1,0:T(8,128)(2,1)}, bf16[128,1024]{1,0:T(8,128)(2,1)}, bf16[512,768]{1,0:T(8,128)(2,1)}, bf16[512,768]{1,0:T(8,128)(2,1)}, bf16[768,512]{1,0:T(8,128)(2,1)}) custom-call(bf16[128,1024]{1,0:T(8,128)(2,1)} %tok.1, bf16[128,1024]{1,0:T(8,128)(2,1)} %cot.1, s32[128,2]{1,0:T(8,128)} %copy.12.ids, f32[128,2]{1,0:T(8,128)} %copy.13.cw, ...), custom_call_target="tpu_custom_call" | custom-call | flops 7247757312 | bytes 6291456 | tf_op jit(solution)/shard_map/pallas_call | solution.py:274
  117.5 0.0 copy-start.2
  117.5 1.7 %copy.19 = bf16[128,1024]{1,0:T(8,128)(2,1)} copy(bf16[128,1024]{1,0:T(8,128)(2,1)} %get-tuple-element.20) | data formatting | bytes 524288
  119.3 1.7 %copy.20 = bf16[128,1024]{1,0:T(8,128)(2,1)} copy(bf16[128,1024]{1,0:T(8,128)(2,1)} %get-tuple-element.21) | data formatting | bytes 524288
  121.0 0.0 copy-done.2
  121.0 0.0 copy-start.1
  121.0 0.9 copy.21
  121.8 0.5 copy-done.1
  122.4 0.0 copy-start
  122.4 0.9 copy.22
  123.3 0.5 copy-done
  123.8 0.9 copy.23
Async XLA Ops:
  0.6 0.7 copy-start.3
  1.3 0.7 copy-start.4
  117.5 3.4 %copy-start.2 = (bf16[512,768]{1,0:T(8,128)(2,1)S(1)}, bf16[512,768]{1,0:T(8,128)(2,1)}, u32[]{:S(2)}) copy-start(bf16[512,768]{1,0:T(8,128)(2,1)} %get-tuple-element.12) | copy-start | bytes 2359300
  121.0 1.4 %copy-start.1 = (bf16[512,768]{1,0:T(8,128)(2,1)S(1)}, bf16[512,768]{1,0:T(8,128)(2,1)}, u32[]{:S(2)}) copy-start(bf16[512,768]{1,0:T(8,128)(2,1)} %get-tuple-element.13) | copy-start | bytes 2359300
  122.4 1.4 %copy-start = (bf16[768,512]{1,0:T(8,128)(2,1)S(1)}, bf16[768,512]{1,0:T(8,128)(2,1)}, u32[]{:S(2)}) copy-start(bf16[768,512]{1,0:T(8,128)(2,1)} %get-tuple-element.14) | copy-start | bytes 2359300

commit v2 on v1

--- a/solution.py
+++ b/solution.py
@@ -28,17 +28,19 @@
 def kernel(
     reps, groups, cap, width,
     tok, cot, ids, cw, wg, wu, wd,
-    mixed, token_grad, gate_grad, up_grad, down_grad,
+    out_mixed, out_tokens, out_gate, out_up, out_down,
     send_x, send_c, send_o, send_d, recv_x, recv_c, recv_o, recv_d,
     full_g, full_u, full_d, hid, d_gate, d_up,
     part_g, part_u, part_d, red_g, red_u, red_d,
     pick, pick_hi, pick_lo,
-    a_send, a_recv, w_send, w_recv, g_send, g_recv, local_sem,
+    flip_x, slope_g, slope_u, mixed, token_grad, gate_grad, up_grad, down_grad,
+    a_send, a_recv, w_send, w_recv, g_send, g_recv, local_sem, out_sem,
 ):
     rep, exp = lax.axis_index("rep"), lax.axis_index("exp")
     tokens, features = tok.shape
     share, hidden = wg.shape
     chunks = hidden // width
+    last = chunks - 1
     rows = groups * cap
     mine = pl.ds(pl.multiple_of(rep * share, share), share)
 
@@ -48,6 +50,10 @@
         return pl.ds(pl.multiple_of(c * width, width), width)
 
     barrier = pltpu.get_barrier_semaphore()
+    for j in range(1, reps):
+        pl.semaphore_signal(
+            barrier, inc=1, device_id=(lax.rem(rep + j, reps), exp), device_id_type=MESH
+        )
 
     def greet(i, carry):
         pl.semaphore_signal(
@@ -56,10 +62,6 @@
         return carry
 
     lax.fori_loop(1, groups, greet, 0)
-    for j in range(1, reps):
-        pl.semaphore_signal(
-            barrier, inc=1, device_id=(lax.rem(rep + j, reps), exp), device_id_type=MESH
-        )
 
     own_copies = [
         pltpu.make_async_copy(wg, full_g.at[mine, :], local_sem.at[0]),
@@ -70,32 +72,21 @@
         copy.start()
 
     lanes = 128
-    expert = lax.broadcasted_iota(jnp.int32, (tokens, lanes), 1)
+    expert = lax.broadcasted_iota(jnp.int32, (lanes, tokens), 0)
     id_val = ids[...]
     cw_val = cw[...]
-    hot = [(id_val[:, k : k + 1] == expert).astype(F32) for k in range(2)]
+    hot = [(id_val[k : k + 1, :] == expert).astype(F32) for k in range(2)]
     earlier = (
-        lax.broadcasted_iota(jnp.int32, (tokens, tokens), 1)
-        < lax.broadcasted_iota(jnp.int32, (tokens, tokens), 0)
-    )
-    before = mm(earlier.astype(F32).astype(BF16), (hot[0] + hot[1]).astype(BF16), NN)
+        lax.broadcasted_iota(jnp.int32, (tokens, tokens), 0)
+        < lax.broadcasted_iota(jnp.int32, (tokens, tokens), 1)
+    )
+    before = mm((hot[0] + hot[1]).astype(BF16), earlier.astype(F32).astype(BF16), NN)
     place = before + (expert * cap).astype(F32)
-    dest = [jnp.sum(hot[k] * place, axis=1, keepdims=True) for k in range(2)]
-    table = jnp.where(
-        expert == 0, dest[0],
-        jnp.where(expert == 1, dest[1],
-                  jnp.where(expert == 2, cw_val[:, 0:1],
-                            jnp.where(expert == 3, cw_val[:, 1:2], 0.0))),
-    )
-    flipped = jnp.transpose(table)
+    dest = [jnp.sum(hot[k] * place, axis=0, keepdims=True) for k in range(2)]
     down_rows = lax.broadcasted_iota(jnp.int32, (rows, tokens), 0).astype(F32)
-    sel0 = (down_rows == flipped[0:1, :]).astype(F32)
-    sel1 = (down_rows == flipped[1:2, :]).astype(F32)
+    sel0 = (down_rows == dest[0]).astype(F32)
+    sel1 = (down_rows == dest[1]).astype(F32)
     select = (sel0 + sel1).astype(BF16)
-    row_weight = jnp.sum(
-        sel0 * flipped[2:3, :] + sel1 * flipped[3:4, :], axis=1, keepdims=True
-    )
-    send_x[...] = mm(select, tok[...], NN).reshape(groups, cap, features).astype(BF16)
 
     pl.semaphore_wait(barrier, groups - 1 + reps - 1)
 
@@ -140,11 +131,12 @@
         )
 
     def start_rows(kind):
-        def step(i, carry):
+        def step(k, carry):
+            i = groups // 2 + (1 - 2 * lax.rem(k, 2)) * ((k + 1) // 2)
             row_copy(kind, i).start()
             return carry
 
-        lax.fori_loop(1, groups, step, 0)
+        lax.fori_loop(0, groups - 1, step, 0)
         src, dst = exchange[kind]
         pltpu.make_async_copy(src.at[exp], dst.at[exp], local_sem.at[3 + kind]).start()
 
@@ -158,20 +150,34 @@
         pltpu.make_async_copy(src.at[exp], dst.at[exp], local_sem.at[3 + kind]).wait()
 
     for c in range(chunks):
-        for a in range(3):
+        for a in range(2):
             for j in range(1, reps):
                 weight_copy(a, c, j).start()
+    for c in range(chunks):
+        for j in range(1, reps):
+            weight_copy(2, c, j).start()
+    send_x[...] = mm(select, tok[...], NN).reshape(groups, cap, features).astype(BF16)
     start_rows(0)
+    row_weight = jnp.sum(
+        sel0 * cw_val[0:1, :] + sel1 * cw_val[1:2, :], axis=1, keepdims=True
+    )
     send_c[...] = (
         (mm(select, cot[...], NN) * row_weight).reshape(groups, cap, features).astype(BF16)
     )
     start_rows(1)
 
+    table = jnp.where(
+        expert == 0, dest[0],
+        jnp.where(expert == 1, dest[1],
+                  jnp.where(expert == 2, cw_val[0:1, :],
+                            jnp.where(expert == 3, cw_val[1:2, :], 0.0))),
+    )
+    flipped = jnp.transpose(table)
     across = lax.broadcasted_iota(jnp.int32, (tokens, rows), 1).astype(F32)
-    at0 = (across == dest[0]).astype(F32)
-    at1 = (across == dest[1]).astype(F32)
+    at0 = (across == flipped[:, 0:1]).astype(F32)
+    at1 = (across == flipped[:, 1:2]).astype(F32)
     pick[...] = (at0 + at1).astype(BF16)
-    weighted = at0 * cw_val[:, 0:1] + at1 * cw_val[:, 1:2]
+    weighted = at0 * flipped[:, 2:3] + at1 * flipped[:, 3:4]
     high = weighted.astype(BF16)
     pick_hi[...] = high
     pick_lo[...] = (weighted - high.astype(F32)).astype(BF16)
@@ -179,70 +185,96 @@
     for copy in own_copies:
         copy.wait()
     finish_rows(0)
-    finish_rows(1)
-
-    def chunk(c, carry):
+    flip_x[...] = jnp.transpose(rows_2d(recv_x[...]))
+
+    def forward(c, carry):
         x = rows_2d(recv_x[...])
         for j in range(1, reps):
-            for a in range(3):
-                weight_copy(a, c, j).wait_recv()
+            weight_copy(0, c, j).wait_recv()
         gate = mm(x, full_g[:, cols(c)], NN)
+        for j in range(1, reps):
+            weight_copy(1, c, j).wait_recv()
         up = mm(x, full_u[:, cols(c)], NN)
-        cots = rows_2d(recv_c[...])
-        grad_h = mm(cots, full_d[cols(c), :], NT)
         sigma = jax.nn.sigmoid(gate)
         swish = gate * sigma
-        h = (swish * up).astype(BF16)
-        dg = (grad_h * up * sigma * (1.0 + gate * (1.0 - sigma))).astype(BF16)
-        du = (grad_h * swish).astype(BF16)
-        hid[:, cols(c)] = h
-        d_gate[:, cols(c)] = dg
-        d_up[:, cols(c)] = du
-        part_g[:, cols(c)] = mm(x, dg, TN).astype(BF16)
+        hid[:, cols(c)] = (swish * up).astype(BF16)
+        slope_u[:, cols(c)] = swish
+        slope_g[:, cols(c)] = up * sigma * (1.0 + gate * (1.0 - sigma))
+        return carry
+
+    def backward(c):
+        grad_h = mm(rows_2d(recv_c[...]), full_d[cols(c), :], NT)
+        d_gate[:, cols(c)] = (grad_h * slope_g[:, cols(c)]).astype(BF16)
+        d_up[:, cols(c)] = (grad_h * slope_u[:, cols(c)]).astype(BF16)
+
+    def gradients(c, carry):
+        part_g[:, cols(c)] = mm(flip_x[...], d_gate[:, cols(c)], NN).astype(BF16)
         for j in range(1, reps):
             grad_copy(0, c, j).start()
-        part_u[:, cols(c)] = mm(x, du, TN).astype(BF16)
+        part_u[:, cols(c)] = mm(flip_x[...], d_up[:, cols(c)], NN).astype(BF16)
         for j in range(1, reps):
             grad_copy(1, c, j).start()
-        part_d[cols(c), :] = mm(h, cots, TN).astype(BF16)
+        part_d[cols(c), :] = mm(hid[:, cols(c)], rows_2d(recv_c[...]), TN).astype(BF16)
         for j in range(1, reps):
             grad_copy(2, c, j).start()
         return carry
 
-    lax.fori_loop(0, chunks, chunk, 0)
-
-    send_o[...] = mm(hid[...], full_d[...], NN).reshape(groups, cap, features).astype(BF16)
-    start_rows(2)
+    lax.fori_loop(0, chunks, forward, 0)
+    finish_rows(1)
+    for c in range(chunks):
+        for j in range(1, reps):
+            weight_copy(2, c, j).wait_recv()
+        if c == last:
+            send_o[...] = (
+                mm(hid[...], full_d[...], NN).reshape(groups, cap, features).astype(BF16)
+            )
+            start_rows(2)
+        backward(c)
+        if c == 0 and last > 0:
+            gradients(0, 0)
     send_d[...] = (
         (mm(d_gate[...], full_g[...], NT) + mm(d_up[...], full_u[...], NT))
         .reshape(groups, cap, features)
         .astype(BF16)
     )
     start_rows(3)
+    lax.fori_loop(min(1, last), chunks, gradients, 0)
+
+    writes = []
+
+    def write(src, dst):
+        copy = pltpu.make_async_copy(src, dst, out_sem.at[len(writes)])
+        copy.start()
+        writes.append(copy)
+
+    def average(c):
+        for a in range(3):
+            for j in range(1, reps):
+                grad_copy(a, c, j).wait_recv()
+            own, red, mean, out = (
+                (part_g, red_g, gate_grad, out_gate),
+                (part_u, red_u, up_grad, out_up),
+                (part_d, red_d, down_grad, out_down),
+            )[a]
+            here, there = ((slice(None), cols(c)), (mine, cols(c)))
+            if a == 2:
+                here, there = ((cols(c), slice(None)), (cols(c), mine))
+            total = own[there].astype(F32)
+            for j in range(1, reps):
+                total = total + red[(j - 1,) + here].astype(F32)
+            mean[here] = (total / reps).astype(BF16)
+            write(mean.at[here], out.at[here])
 
     finish_rows(2)
     back = rows_2d(recv_o[...])
     mixed[...] = (mm(pick_hi[...], back, NN) + mm(pick_lo[...], back, NN)).astype(BF16)
+    write(mixed, out_mixed)
+    for c in range(last):
+        average(c)
     finish_rows(3)
     token_grad[...] = mm(pick[...], rows_2d(recv_d[...]), NN).astype(BF16)
-
-    for c in range(chunks):
-        for a in range(3):
-            for j in range(1, reps):
-                grad_copy(a, c, j).wait_recv()
-            own, red, out = (
-                (part_g, red_g, gate_grad), (part_u, red_u, up_grad), (part_d, red_d, down_grad)
-            )[a]
-            if a < 2:
-                total = own[mine, cols(c)].astype(F32)
-                for j in range(1, reps):
-                    total = total + red[j - 1, :, cols(c)].astype(F32)
-                out[:, cols(c)] = (total / reps).astype(BF16)
-            else:
-                total = own[cols(c), mine].astype(F32)
-                for j in range(1, reps):
-                    total = total + red[j - 1, cols(c), :].astype(F32)
-                out[cols(c), :] = (total / reps).astype(BF16)
+    write(token_grad, out_tokens)
+    average(last)
 
     for c in range(chunks):
         for a in range(3):
@@ -256,6 +288,19 @@
         return carry
 
     lax.fori_loop(1, groups, sent, 0)
+    for copy in writes:
+        copy.wait()
+
+
+def hand_out(count, *refs):
+    sems = refs[-1]
+    copies = [
+        pltpu.make_async_copy(refs[k], refs[count + k], sems.at[k]) for k in range(count)
+    ]
+    for copy in copies:
+        copy.start()
+    for copy in copies:
+        copy.wait()
 
 
 def per_device(reps, groups, tokens, cotangent, expert_ids, combine_weight, gate_w, up_w, down_w):
@@ -267,21 +312,23 @@
     width = 256
     chunks = hidden // width
     vmem = pl.BlockSpec(memory_space=pltpu.VMEM)
+    anywhere = pl.BlockSpec(memory_space=pl.ANY)
     block = pltpu.VMEM((groups, cap, features), BF16)
     act = pltpu.VMEM((rows, hidden), BF16)
     dma = pltpu.SemaphoreType.DMA
     others = reps - 1
+    shapes = (
+        jax.ShapeDtypeStruct((tok_rows, features), BF16),
+        jax.ShapeDtypeStruct((tok_rows, features), BF16),
+        jax.ShapeDtypeStruct((share, hidden), BF16),
+        jax.ShapeDtypeStruct((share, hidden), BF16),
+        jax.ShapeDtypeStruct((hidden, share), BF16),
+    )
     outs = pl.pallas_call(
         functools.partial(kernel, reps, groups, cap, width),
-        out_shape=(
-            jax.ShapeDtypeStruct((tok_rows, features), BF16),
-            jax.ShapeDtypeStruct((tok_rows, features), BF16),
-            jax.ShapeDtypeStruct((share, hidden), BF16),
-            jax.ShapeDtypeStruct((share, hidden), BF16),
-            jax.ShapeDtypeStruct((hidden, share), BF16),
-        ),
-        in_specs=[vmem] * 7,
-        out_specs=(vmem,) * 5,
+        out_shape=shapes,
+        in_specs=[vmem] * 4 + [anywhere] * 3,
+        out_specs=(anywhere,) * 5,
         scratch_shapes=[block] * 8
         + [
             pltpu.VMEM((features, hidden), BF16),
@@ -298,6 +345,9 @@
             pltpu.VMEM((others, hidden, share), BF16),
         ]
         + [pltpu.VMEM((tok_rows, rows), BF16)] * 3
+        + [pltpu.VMEM((features, rows), BF16)]
+        + [pltpu.VMEM((rows, hidden), F32)] * 2
+        + [pltpu.VMEM(shape.shape, BF16) for shape in shapes]
         + [
             dma((4, groups - 1)),
             dma((4, groups - 1)),
@@ -306,6 +356,7 @@
             dma((others, 3, chunks)),
             dma((others, 3, chunks)),
             dma((7,)),
+            dma((2 + 3 * chunks,)),
         ],
         compiler_params=pltpu.CompilerParams(
             collective_id=0, has_side_effects=True, vmem_limit_bytes=56 * 1024 * 1024
@@ -315,8 +366,15 @@
             bytes_accessed=16 * share * hidden,
             transcendentals=rows * hidden,
         ),
-    )(tokens, cotangent, expert_ids, combine_weight, gate_w[0], up_w[0], down_w[0])
-    mixed, token_grad, gate_grad, up_grad, down_grad = outs
+    )(tokens, cotangent, expert_ids.T, combine_weight.T, gate_w[0], up_w[0], down_w[0])
+    mixed, token_grad, gate_grad, up_grad, down_grad = pl.pallas_call(
+        functools.partial(hand_out, len(shapes)),
+        out_shape=shapes,
+        in_specs=[anywhere] * len(shapes),
+        out_specs=(anywhere,) * len(shapes),
+        scratch_shapes=[dma((len(shapes),))],
+        compiler_params=pltpu.CompilerParams(vmem_limit_bytes=60 * 1024 * 1024),
+    )(*outs)
     return mixed, token_grad, gate_grad[None], up_grad[None], down_grad[None]
 
 

time: 125 us -> 203 us (1.62)
  Pallas kernels: 115 us -> 202 us
  local copies, waits for them, and re-layouts: 9.28 us -> 0 us
    pallas_call x0 -> x1, Pallas kernels: none -> 88.5 us  [per_device(): pl.pallas_call(functools.partial(hand_out, len(shapes)), out_shape=shapes...]
    unnamed x17 -> x0, local copies, waits for them, and re-layouts: 9.28 us -> none
where the time goes in v2:
time: 203 us; the launch traced here: 202 us
  Pallas kernels  202 us (100%)
    pallas_call x1, Pallas kernels, per_device(): pl.pallas_call(functools.partial(kernel, reps, groups, cap, width), out_s...  113 us
    pallas_call x1, Pallas kernels, per_device(): pl.pallas_call(functools.partial(hand_out, len(shapes)), out_shape=shapes...  88.5 us

profile of v2, /device:TPU:0, one launch (start us, length us, event | category | flops | bytes accessed | tf_op | source)
XLA Modules:
  0.0 202.4 jit_solution(18137306178842456341)
XLA Ops:
  0.6 113.2 %shard_map.110 = (bf16[128,1024]{1,0:T(8,128)(2,1)}, bf16[128,1024]{1,0:T(8,128)(2,1)}, bf16[512,768]{1,0:T(8,128)(2,1)}, bf16[512,768]{1,0:T(8,128)(2,1)}, bf16[768,512]{1,0:T(8,128)(2,1)}) custom-call(bf16[128,1024]{1,0:T(8,128)(2,1)} %tok.1, bf16[128,1024]{1,0:T(8,128)(2,1)} %cot.1, s32[2,128]{1,0:T(2,128)} %bitcast.14, f32[2,128]{1,0:T(2,128)} %bitcast.15, ...), custom_call_target="tpu_custom_call" | custom-call | flops 7247757312 | bytes 6291456 | tf_op jit(solution)/shard_map/pallas_call | solution.py:327
  113.9 88.5 %shard_map.111 = (bf16[128,1024]{1,0:T(8,128)(2,1)}, bf16[128,1024]{1,0:T(8,128)(2,1)}, bf16[512,768]{1,0:T(8,128)(2,1)}, bf16[512,768]{1,0:T(8,128)(2,1)}, bf16[768,512]{1,0:T(8,128)(2,1)}) custom-call(bf16[128,1024]{1,0:T(8,128)(2,1)} %get-tuple-element.15.refs_0_, bf16[128,1024]{1,0:T(8,128)(2,1)} %get-tuple-element.16.refs_1_, ...), custom_call_target="tpu_custom_call" | custom-call | tf_op jit(solution)/shard_map/pallas_call | solution.py:370

commit v3 on v2

--- a/solution.py
+++ b/solution.py
@@ -293,14 +293,21 @@
 
 
 def hand_out(count, *refs):
+    sources, targets, stages = refs[:count], refs[count : 2 * count], refs[2 * count : 3 * count]
     sems = refs[-1]
-    copies = [
-        pltpu.make_async_copy(refs[k], refs[count + k], sems.at[k]) for k in range(count)
+    loads = [
+        pltpu.make_async_copy(sources[k], stages[k], sems.at[0, k]) for k in range(count)
     ]
-    for copy in copies:
-        copy.start()
-    for copy in copies:
-        copy.wait()
+    stores = [
+        pltpu.make_async_copy(stages[k], targets[k], sems.at[1, k]) for k in range(count)
+    ]
+    for load in loads:
+        load.start()
+    for load, store in zip(loads, stores):
+        load.wait()
+        store.start()
+    for store in stores:
+        store.wait()
 
 
 def per_device(reps, groups, tokens, cotangent, expert_ids, combine_weight, gate_w, up_w, down_w):
@@ -372,7 +379,7 @@
         out_shape=shapes,
         in_specs=[anywhere] * len(shapes),
         out_specs=(anywhere,) * len(shapes),
-        scratch_shapes=[dma((len(shapes),))],
+        scratch_shapes=[pltpu.VMEM(shape.shape, BF16) for shape in shapes] + [dma((2, len(shapes)))],
         compiler_params=pltpu.CompilerParams(vmem_limit_bytes=60 * 1024 * 1024),
     )(*outs)
     return mixed, token_grad, gate_grad[None], up_grad[None], down_grad[None]

time: 203 us -> 117 us (0.58)
  Pallas kernels: 202 us -> 116 us
    pallas_call x1, Pallas kernels: 88.5 us -> 2.78 us  [per_device(): pl.pallas_call(functools.partial(hand_out, len(shapes)), out_shape=shapes...]
where the time goes in v3:
time: 117 us
  Pallas kernels  116 us (99%)
    pallas_call x1, Pallas kernels, per_device(): pl.pallas_call(functools.partial(kernel, reps, groups, cap, width), out_s...  113 us
    pallas_call x1, Pallas kernels, per_device(): pl.pallas_call(functools.partial(hand_out, len(shapes)), out_shape=shapes...  2.78 us

profile of v3, /device:TPU:0, one launch (start us, length us, event | category | flops | bytes accessed | tf_op | source)
XLA Modules:
  0.0 116.7 jit_solution(6026164852540372433)
XLA Ops:
  0.6 113.2 %shard_map.110 = (bf16[128,1024]{1,0:T(8,128)(2,1)}, bf16[128,1024]{1,0:T(8,128)(2,1)}, bf16[512,768]{1,0:T(8,128)(2,1)}, bf16[512,768]{1,0:T(8,128)(2,1)}, bf16[768,512]{1,0:T(8,128)(2,1)}) custom-call(bf16[128,1024]{1,0:T(8,128)(2,1)} %tok.1, bf16[128,1024]{1,0:T(8,128)(2,1)} %cot.1, s32[2,128]{1,0:T(2,128)} %bitcast.14, f32[2,128]{1,0:T(2,128)} %bitcast.15, ...), custom_call_target="tpu_custom_call" | custom-call | flops 7247757312 | bytes 6291456 | tf_op jit(solution)/shard_map/pallas_call | solution.py:334
  113.9 2.8 %shard_map.111 = (bf16[128,1024]{1,0:T(8,128)(2,1)}, bf16[128,1024]{1,0:T(8,128)(2,1)}, bf16[512,768]{1,0:T(8,128)(2,1)}, bf16[512,768]{1,0:T(8,128)(2,1)}, bf16[768,512]{1,0:T(8,128)(2,1)}) custom-call(bf16[128,1024]{1,0:T(8,128)(2,1)} %get-tuple-element.15.refs_0_, bf16[128,1024]{1,0:T(8,128)(2,1)} %get-tuple-element.16.refs_1_, ...), custom_call_target="tpu_custom_call" | custom-call | tf_op jit(solution)/shard_map/pallas_call | solution.py:377

commit v4 on v3

--- a/solution.py
+++ b/solution.py
@@ -27,17 +27,18 @@
 
 def kernel(
     reps, groups, cap, width,
-    tok, cot, ids, cw, wg, wu, wd,
+    tok_in, cot_in, ids_in, cw_in, wg, wu, wd,
     out_mixed, out_tokens, out_gate, out_up, out_down,
     send_x, send_c, send_o, send_d, recv_x, recv_c, recv_o, recv_d,
     full_g, full_u, full_d, hid, d_gate, d_up,
     part_g, part_u, part_d, red_g, red_u, red_d,
     pick, pick_hi, pick_lo,
     flip_x, slope_g, slope_u, mixed, token_grad, gate_grad, up_grad, down_grad,
+    tok, cot, ids, cw,
     a_send, a_recv, w_send, w_recv, g_send, g_recv, local_sem, out_sem,
 ):
     rep, exp = lax.axis_index("rep"), lax.axis_index("exp")
-    tokens, features = tok.shape
+    tokens, features = tok_in.shape
     share, hidden = wg.shape
     chunks = hidden // width
     last = chunks - 1
@@ -63,31 +64,12 @@
 
     lax.fori_loop(1, groups, greet, 0)
 
-    own_copies = [
-        pltpu.make_async_copy(wg, full_g.at[mine, :], local_sem.at[0]),
-        pltpu.make_async_copy(wu, full_u.at[mine, :], local_sem.at[1]),
-        pltpu.make_async_copy(wd, full_d.at[:, mine], local_sem.at[2]),
+    loads = [
+        pltpu.make_async_copy(src, dst, local_sem.at[7 + k])
+        for k, (src, dst) in enumerate(((ids_in, ids), (cw_in, cw), (tok_in, tok), (cot_in, cot)))
     ]
-    for copy in own_copies:
-        copy.start()
-
-    lanes = 128
-    expert = lax.broadcasted_iota(jnp.int32, (lanes, tokens), 0)
-    id_val = ids[...]
-    cw_val = cw[...]
-    hot = [(id_val[k : k + 1, :] == expert).astype(F32) for k in range(2)]
-    earlier = (
-        lax.broadcasted_iota(jnp.int32, (tokens, tokens), 0)
-        < lax.broadcasted_iota(jnp.int32, (tokens, tokens), 1)
-    )
-    before = mm((hot[0] + hot[1]).astype(BF16), earlier.astype(F32).astype(BF16), NN)
-    place = before + (expert * cap).astype(F32)
-    dest = [jnp.sum(hot[k] * place, axis=0, keepdims=True) for k in range(2)]
-    down_rows = lax.broadcasted_iota(jnp.int32, (rows, tokens), 0).astype(F32)
-    sel0 = (down_rows == dest[0]).astype(F32)
-    sel1 = (down_rows == dest[1]).astype(F32)
-    select = (sel0 + sel1).astype(BF16)
-
+    for load in loads:
+        load.start()
     pl.semaphore_wait(barrier, groups - 1 + reps - 1)
 
     def weight_copy(a, c, j):
@@ -105,6 +87,41 @@
             device_id=(peer, exp), device_id_type=MESH,
         )
 
+    for c in range(chunks):
+        for a in range(2):
+            for j in range(1, reps):
+                weight_copy(a, c, j).start()
+    for c in range(chunks):
+        for j in range(1, reps):
+            weight_copy(2, c, j).start()
+
+    own_copies = [
+        pltpu.make_async_copy(wg, full_g.at[mine, :], local_sem.at[0]),
+        pltpu.make_async_copy(wu, full_u.at[mine, :], local_sem.at[1]),
+        pltpu.make_async_copy(wd, full_d.at[:, mine], local_sem.at[2]),
+    ]
+    for copy in own_copies:
+        copy.start()
+
+    lanes = 128
+    expert = lax.broadcasted_iota(jnp.int32, (lanes, tokens), 0)
+    loads[0].wait()
+    loads[1].wait()
+    id_val = ids[...]
+    cw_val = cw[...]
+    hot = [(id_val[k : k + 1, :] == expert).astype(F32) for k in range(2)]
+    earlier = (
+        lax.broadcasted_iota(jnp.int32, (tokens, tokens), 0)
+        < lax.broadcasted_iota(jnp.int32, (tokens, tokens), 1)
+    )
+    before = mm((hot[0] + hot[1]).astype(BF16), earlier.astype(F32).astype(BF16), NN)
+    place = before + (expert * cap).astype(F32)
+    dest = [jnp.sum(hot[k] * place, axis=0, keepdims=True) for k in range(2)]
+    down_rows = lax.broadcasted_iota(jnp.int32, (rows, tokens), 0).astype(F32)
+    sel0 = (down_rows == dest[0]).astype(F32)
+    sel1 = (down_rows == dest[1]).astype(F32)
+    select = (sel0 + sel1).astype(BF16)
+
     def grad_copy(a, c, j):
         peer = lax.rem(rep + j, reps)
         theirs = pl.ds(pl.multiple_of(peer * share, share), share)
@@ -149,18 +166,13 @@
         src, dst = exchange[kind]
         pltpu.make_async_copy(src.at[exp], dst.at[exp], local_sem.at[3 + kind]).wait()
 
-    for c in range(chunks):
-        for a in range(2):
-            for j in range(1, reps):
-                weight_copy(a, c, j).start()
-    for c in range(chunks):
-        for j in range(1, reps):
-            weight_copy(2, c, j).start()
+    loads[2].wait()
     send_x[...] = mm(select, tok[...], NN).reshape(groups, cap, features).astype(BF16)
     start_rows(0)
     row_weight = jnp.sum(
         sel0 * cw_val[0:1, :] + sel1 * cw_val[1:2, :], axis=1, keepdims=True
     )
+    loads[3].wait()
     send_c[...] = (
         (mm(select, cot[...], NN) * row_weight).reshape(groups, cap, features).astype(BF16)
     )
@@ -265,42 +277,57 @@
             mean[here] = (total / reps).astype(BF16)
             write(mean.at[here], out.at[here])
 
+    def grads_sent(c):
+        for a in range(3):
+            for j in range(1, reps):
+                grad_copy(a, c, j).wait_send()
+
+    def rows_sent(kind):
+        def step(i, carry):
+            row_copy(kind, i).wait_send()
+            return carry
+
+        lax.fori_loop(1, groups, step, 0)
+
+    rows_sent(0)
+    rows_sent(1)
+    for c in range(chunks):
+        for a in range(3):
+            for j in range(1, reps):
+                weight_copy(a, c, j).wait_send()
     finish_rows(2)
     back = rows_2d(recv_o[...])
     mixed[...] = (mm(pick_hi[...], back, NN) + mm(pick_lo[...], back, NN)).astype(BF16)
     write(mixed, out_mixed)
     for c in range(last):
         average(c)
+        grads_sent(c)
+    rows_sent(2)
     finish_rows(3)
     token_grad[...] = mm(pick[...], rows_2d(recv_d[...]), NN).astype(BF16)
     write(token_grad, out_tokens)
+    rows_sent(3)
     average(last)
 
-    for c in range(chunks):
-        for a in range(3):
-            for j in range(1, reps):
-                weight_copy(a, c, j).wait_send()
-                grad_copy(a, c, j).wait_send()
-
-    def sent(i, carry):
-        for kind in range(4):
-            row_copy(kind, i).wait_send()
-        return carry
-
-    lax.fori_loop(1, groups, sent, 0)
+    grads_sent(last)
     for copy in writes:
         copy.wait()
 
 
-def hand_out(count, *refs):
+def hand_out(count, pieces, *refs):
     sources, targets, stages = refs[:count], refs[count : 2 * count], refs[2 * count : 3 * count]
     sems = refs[-1]
-    loads = [
-        pltpu.make_async_copy(sources[k], stages[k], sems.at[0, k]) for k in range(count)
-    ]
-    stores = [
-        pltpu.make_async_copy(stages[k], targets[k], sems.at[1, k]) for k in range(count)
-    ]
+    loads, stores = [], []
+    for k in reversed(range(count)):
+        size = sources[k].shape[0] // pieces
+        for p in range(pieces):
+            part, at = pl.ds(p * size, size), k * pieces + p
+            loads.append(
+                pltpu.make_async_copy(sources[k].at[part], stages[k].at[part], sems.at[0, at])
+            )
+            stores.append(
+                pltpu.make_async_copy(stages[k].at[part], targets[k].at[part], sems.at[1, at])
+            )
     for load in loads:
         load.start()
     for load, store in zip(loads, stores):
@@ -318,7 +345,7 @@
     rows = groups * cap
     width = 256
     chunks = hidden // width
-    vmem = pl.BlockSpec(memory_space=pltpu.VMEM)
+    pieces = 4
     anywhere = pl.BlockSpec(memory_space=pl.ANY)
     block = pltpu.VMEM((groups, cap, features), BF16)
     act = pltpu.VMEM((rows, hidden), BF16)
@@ -334,7 +361,7 @@
     outs = pl.pallas_call(
         functools.partial(kernel, reps, groups, cap, width),
         out_shape=shapes,
-        in_specs=[vmem] * 4 + [anywhere] * 3,
+        in_specs=[anywhere] * 7,
         out_specs=(anywhere,) * 5,
         scratch_shapes=[block] * 8
         + [
@@ -356,13 +383,19 @@
         + [pltpu.VMEM((rows, hidden), F32)] * 2
         + [pltpu.VMEM(shape.shape, BF16) for shape in shapes]
         + [
+            pltpu.VMEM((tok_rows, features), BF16),
+            pltpu.VMEM((tok_rows, features), BF16),
+            pltpu.VMEM((top, tok_rows), jnp.int32),
+            pltpu.VMEM((top, tok_rows), F32),
+        ]
+        + [
             dma((4, groups - 1)),
             dma((4, groups - 1)),
             dma((others, 3, chunks)),
             dma((others, 3, chunks)),
             dma((others, 3, chunks)),
             dma((others, 3, chunks)),
-            dma((7,)),
+            dma((11,)),
             dma((2 + 3 * chunks,)),
         ],
         compiler_params=pltpu.CompilerParams(
@@ -375,11 +408,11 @@
         ),
     )(tokens, cotangent, expert_ids.T, combine_weight.T, gate_w[0], up_w[0], down_w[0])
     mixed, token_grad, gate_grad, up_grad, down_grad = pl.pallas_call(
-        functools.partial(hand_out, len(shapes)),
+        functools.partial(hand_out, len(shapes), pieces),
         out_shape=shapes,
         in_specs=[anywhere] * len(shapes),
         out_specs=(anywhere,) * len(shapes),
-        scratch_shapes=[pltpu.VMEM(shape.shape, BF16) for shape in shapes] + [dma((2, len(shapes)))],
+        scratch_shapes=[pltpu.VMEM(shape.shape, BF16) for shape in shapes] + [dma((2, len(shapes) * pieces))],
         compiler_params=pltpu.CompilerParams(vmem_limit_bytes=60 * 1024 * 1024),
     )(*outs)
     return mixed, token_grad, gate_grad[None], up_grad[None], down_grad[None]

time: 117 us -> 116 us (level)
  no operation moved by 1% of the time
where the time goes in v4:
time: 116 us
  Pallas kernels  115 us (99%)
    pallas_call x1, Pallas kernels, per_device(): pl.pallas_call(functools.partial(kernel, reps, groups, cap, width), out_s...  112 us
    pallas_call x1, Pallas kernels, per_device(): pl.pallas_call(functools.partial(hand_out, len(shapes), pieces), out_shap...  2.93 us

profile of v4, /device:TPU:0, one launch (start us, length us, event | category | flops | bytes accessed | tf_op | source)
XLA Modules:
  0.0 115.9 jit_solution(13293119197445799495)
XLA Ops:
  0.6 112.3 %shard_map.110 = (bf16[128,1024]{1,0:T(8,128)(2,1)}, bf16[128,1024]{1,0:T(8,128)(2,1)}, bf16[512,768]{1,0:T(8,128)(2,1)}, bf16[512,768]{1,0:T(8,128)(2,1)}, bf16[768,512]{1,0:T(8,128)(2,1)}) custom-call(bf16[128,1024]{1,0:T(8,128)(2,1)} %tok_in.1, bf16[128,1024]{1,0:T(8,128)(2,1)} %cot_in.1, s32[2,128]{1,0:T(2,128)} %bitcast.14, f32[2,128]{1,0:T(2,128)} %bitcast.15, ...), custom_call_target="tpu_custom_call" | custom-call | flops 7247757312 | bytes 6291456 | tf_op jit(solution)/shard_map/pallas_call | solution.py:361
  112.9 2.9 %shard_map.111 = (bf16[128,1024]{1,0:T(8,128)(2,1)}, bf16[128,1024]{1,0:T(8,128)(2,1)}, bf16[512,768]{1,0:T(8,128)(2,1)}, bf16[512,768]{1,0:T(8,128)(2,1)}, bf16[768,512]{1,0:T(8,128)(2,1)}) custom-call(bf16[128,1024]{1,0:T(8,128)(2,1)} %get-tuple-element.15.refs_0_, bf16[128,1024]{1,0:T(8,128)(2,1)} %get-tuple-element.16.refs_1_, ...), custom_call_target="tpu_custom_call" | custom-call | tf_op jit(solution)/shard_map/pallas_call | solution.py:410
